TPU v7x, 256 devices: a whole 4x4x8 slice. The times are simulated.
256 devices in a mesh: row: 16 (over y, x_hi, core), col: 16 (over z, x_lo).
Axes of the slice: x: 4 (x_hi: 2, x_lo: 2; x = x_hi * 2 + x_lo), y: 4, z: 8, core: 2. Of those that a mesh axis runs over, the one named last changes fastest.
Arguments:
- iterate: bfloat16 [1, 4608, 18432], P(None, 'row', 'col'), may hold values from -0.03125 to 0.03125
- weights: float32 [1, 4608, 18432], P(None, 'row', 'col'), may hold values from -6 to 6
Outputs:
- update: bfloat16 [1, 4608, 18432], P(None, 'row', 'col')
- new_weights: float32 [1, 4608, 18432], P(None, 'row', 'col')
All inputs are finite; a program needn't handle non-finite values.
Results may differ from a plain program's by a relative error of at most 0.0064.
Values may be sent and summed in bfloat16 or wider, within the bound.
A program may use at most 64 MiB of HBM per device.

v0:
```python
import math

import jax
import jax.numpy as jnp
from jax import lax
from jax.sharding import PartitionSpec as P

FFN = 18432


coef_linear = 3.4445
coef_cubic = -4.775
coef_quintic = 2.0315
step_size = 0.02


def per_device(iterate, weights):
    own_tile = iterate[0]
    partial_strip = lax.dot_general(
        own_tile,
        lax.all_gather(own_tile, "row", axis=0, tiled=True),
        (((1,), (1,)), ((), ())),
        preferred_element_type=jnp.float32,
    )
    gram_block = lax.psum_scatter(partial_strip, "col", scatter_dimension=1, tiled=True)
    block_low = gram_block.astype(jnp.bfloat16)
    strip_low = lax.all_gather(block_low, "col", axis=1, tiled=True)
    left_part = strip_low
    square_block = jnp.dot(
        left_part,
        lax.all_gather(block_low, "row", axis=0, tiled=True),
        preferred_element_type=jnp.float32,
    )
    poly_block = (coef_cubic * gram_block + coef_quintic * square_block).astype(jnp.bfloat16)
    poly_strip = lax.all_gather(poly_block, "col", axis=1, tiled=True)
    left_part = poly_strip
    product = jnp.dot(
        left_part,
        lax.all_gather(own_tile, "row", axis=0, tiled=True),
        preferred_element_type=jnp.float32,
    )
    update = (math.sqrt(FFN) * (coef_linear * own_tile.astype(jnp.float32) + product)).astype(
        jnp.bfloat16
    )
    new_layer = weights[0] - step_size * update.astype(jnp.float32)
    updates = [update]
    layers_new = [new_layer]
    return (jnp.stack(updates), jnp.stack(layers_new))


def solution(mesh):
    return jax.shard_map(
        per_device,
        mesh=mesh,
        in_specs=(P(None, "row", "col"), P(None, "row", "col")),
        out_specs=(P(None, "row", "col"), P(None, "row", "col")),
        check_vma=False,
    )
```

profile of v0, /device:TPU:1, one launch (start us, length us, event | category | flops | bytes accessed | tf_op | source)
XLA Modules:
  0.0 523.6 jit_solution(1438770177604687275)
XLA Ops:
  7.2 0.0 all-gather.12.cloned.1.call-start
  7.2 0.7 all-gather.12.cloned.1.call-update
  7.9 0.0 reduce-scatter.4.cloned.1.call-start
  7.9 94.5 %all-gather.12.cloned.1.call-done = bf16[1,4608,1152]{2,1,0:T(8,128)(2,1)} async-done(((bf16[1,288,1152]{2,1,0:T(8,128)(2,1)}), bf16[1,4608,1152]{2,1,0:T(8,128)(2,1)}) %all-gather.12.cloned.1.call-update) | async-done | bytes 10616848 | tf_op jit(solution)/shard_map/all_gather | solution.py:21
  102.5 10.6 %fusion.4 = f32[4608,288]{1,0:T(8,128)} fusion(bf16[1,4608,1152]{2,1,0:T(8,128)(2,1)} %all-gather.12.cloned.1.call-done, bf16[1,288,1152]{2,1,0:T(8,128)(2,1)} %param.2), kind=kOutput, calls=%fused_computation.4 | convolution fusion | flops 3057647616 | bytes 16588800
  113.1 0.0 reduce-scatter.4.cloned.1.call-update
  113.1 0.0 all-gather.8.cloned.1.call-start
  113.1 153.6 %reduce-scatter.4.cloned.1.call-done = f32[288,288]{1,0:T(8,128)} async-done(((f32[4608,288]{1,0:T(8,128)}), f32[288,288]{1,0:T(8,128)}) %reduce-scatter.4.cloned.1.call-update) | async-done | bytes 331792
  266.8 1.2 copy.7
  268.0 0.7 convert_element_type.16
  268.7 0.0 all-gather.8.cloned.1.call-update
  268.7 0.0 all-gather.6.cloned.1.call-start
  268.8 1.8 copy.4
  270.5 0.0 all-gather.6.cloned.1.call-update
  270.6 0.0 copy-start.1
  270.6 0.0 all-gather.10.cloned.1.call-start
  270.6 58.8 %all-gather.8.cloned.1.call-done = bf16[4608,288]{1,0:T(8,128)(2,1)} async-done(((bf16[288,288]{1,0:T(8,128)(2,1)}), bf16[4608,288]{1,0:T(8,128)(2,1)}) %all-gather.8.cloned.1.call-update) | async-done | bytes 2654224 | tf_op jit(solution)/shard_map/all_gather | solution.py:31
  329.4 85.1 %all-gather.6.cloned.1.call-done = bf16[288,4608]{0,1:T(8,128)(2,1)} async-done(((bf16[288,288]{0,1:T(8,128)(2,1)}), bf16[288,4608]{0,1:T(8,128)(2,1)}) %all-gather.6.cloned.1.call-update) | async-done | bytes 2654224 | tf_op jit(solution)/shard_map/all_gather | solution.py:27
  414.5 4.6 fusion.18
  419.2 0.8 copy.5
  420.0 0.0 all-gather.10.cloned.1.call-update
  420.1 0.0 copy-start.2
  420.1 87.0 %all-gather.10.cloned.1.call-done = bf16[288,4608]{0,1:T(8,128)(2,1)} async-done(((bf16[288,288]{0,1:T(8,128)(2,1)}), bf16[288,4608]{0,1:T(8,128)(2,1)}) %all-gather.10.cloned.1.call-update) | async-done | bytes 2654224 | tf_op jit(solution)/shard_map/all_gather | solution.py:35
  507.1 0.0 copy-done.1
  507.1 8.7 %fusion.13 = bf16[288,1152]{1,0:T(8,128)(2,1)S(1)} fusion(bf16[288,4608]{0,1:T(8,128)(2,1)} %all-gather.10.cloned.1.call-done, bf16[1,4608,1152]{2,1,0:T(8,128)(2,1)} %all-gather.12.cloned.1.call-done, bf16[1,288,1152]{2,1,0:T(8,128)(2,1)S(1)} %copy-done.1), kind=kOutput, calls=%fused_computation.7 | convolution fusion | flops 3059306496 | bytes 14598144 | tf_op jit(solution)/shard_map/dot_general | solution.py:37
  515.8 0.0 copy-done.2
  515.8 0.0 copy-start
  515.8 1.3 fusion.16
  517.1 0.0 copy-done
Async XLA Ops:
  7.2 95.3 %all-gather.12.cloned.1.call-start = ((), (), s32[]{:S(2)}) async-start(), calls=%async_computation.4 | async-start | bytes 11280384 | tf_op jit(solution)/shard_map/all_gather | solution.py:21
  7.9 258.9 %reduce-scatter.4.cloned.1.call-start = ((), (), s32[]{:S(2)}) async-start(), calls=%async_computation.5 | async-start | bytes 7520256
  113.1 216.3 %all-gather.8.cloned.1.call-start = ((), (), s32[]{:S(2)}) async-start(), calls=%async_computation.2 | async-start | bytes 3760128 | tf_op jit(solution)/shard_map/all_gather | solution.py:31
  268.7 145.8 %all-gather.6.cloned.1.call-start = ((), (), s32[]{:S(2)}) async-start(), calls=%async_computation.1 | async-start | bytes 3760128 | tf_op jit(solution)/shard_map/all_gather | solution.py:27
  270.6 236.5 %copy-start.1 = (bf16[1,288,1152]{2,1,0:T(8,128)(2,1)S(1)}, bf16[1,288,1152]{2,1,0:T(8,128)(2,1)}, u32[]{:S(2)}) copy-start(bf16[1,288,1152]{2,1,0:T(8,128)(2,1)} %param.2) | copy-start | bytes 1990660
  270.6 236.5 %all-gather.10.cloned.1.call-start = ((), (), s32[]{:S(2)}) async-start(), calls=%async_computation.3 | async-start | bytes 3760128 | tf_op jit(solution)/shard_map/all_gather | solution.py:35
  420.1 95.8 %copy-start.2 = (f32[1,288,1152]{2,1,0:T(8,128)S(1)}, f32[1,288,1152]{2,1,0:T(8,128)}, u32[]{:S(2)}) copy-start(f32[1,288,1152]{2,1,0:T(8,128)} %param.3) | copy-start | bytes 3981316
  515.8 1.3 copy-start
Sparse Core Ops, SparseCore 0:
  10.8 91.6 all-gather.11
  113.2 153.4 reduce-scatter.3
  270.5 58.8 all-gather.7
  331.8 82.7 all-gather.5
  420.2 86.8 all-gather.9
where the time goes:
time: 527 us; the launch traced here: 524 us
  waiting for transfers between devices  480 us (91%)
  matrix products  24 us (5%)
  between operations  13.8 us (3%)
    unnamed x6, waiting for transfers between devices  154 us
    all_gather x1, waiting for transfers between devices, per_device(): lax.all_gather(own_tile, 'row', axis=0, tiled=True)  94.5 us
    all_gather x1, waiting for transfers between devices, per_device(): poly_strip = lax.all_gather(poly_block, 'col', axis=1, tiled=True)  87 us
    all_gather x1, waiting for transfers between devices, per_device(): strip_low = lax.all_gather(block_low, 'col', axis=1, tiled=True)  85.1 us
    all_gather x1, waiting for transfers between devices, per_device(): lax.all_gather(block_low, 'row', axis=0, tiled=True)  58.8 us
    unnamed x1, matrix products  10.6 us
  transfers between devices with their start and end apart: 5, of which 5 were waited for; matrix products, arithmetic and copies ran while one was open for 0% of the time, Pallas kernels for 0%

commit v1 on v0

v1 whole, which is shorter than its diff:
```python
import functools
import math

import jax
import jax.numpy as jnp
from jax import lax
from jax.experimental import pallas as pl
from jax.experimental.pallas import tpu as pltpu
from jax.sharding import PartitionSpec as P

MESH = pl.DeviceIdType.MESH

FFN = 18432
coef_linear = 3.4445
coef_cubic = -4.775
coef_quintic = 2.0315
step_size = 0.02

T = 288
H = 144
N = 1152
S = 72
C = 384
NC = N // C
N_COPIES = 96

SLOT = {(0, 0): 0, (0, 1): 1, (1, 0): 2, (1, 1): 3, (3, 0): 4, (3, 1): 5, (2, 0): 6, (2, 1): 7}


def nt(a, b):
    return lax.dot_general(a, b, (((1,), (1,)), ((), ())), preferred_element_type=jnp.float32)


def kernel(
    x_ref, w_ref, upd_ref, new_ref,
    xb, xp, gp, stage, rs, xs, xr, ga, gs, yo, ys, yr, vb, zo, zs, zr, ssem, rsem,
):
    r, c = lax.axis_index("row"), lax.axis_index("col")
    core, xh, y = lax.rem(r, 2), lax.rem(r // 2, 2), r // 4
    xl, z = lax.rem(c, 2), c // 2

    def at(y_, xh_, core_, z_, xl_):
        return ((y_ * 2 + xh_) * 2 + core_, z_ * 2 + xl_)

    up = at(lax.rem(y + 1, 4), xh, core, z, xl)
    down = at(lax.rem(y + 3, 4), xh, core, z, xl)
    across = at(y, 1 - xh, core, z, xl)
    other = at(y, xh, 1 - core, z, xl)
    right = at(y, xh, core, lax.rem(z + 1, 8), xl)
    left = at(y, xh, core, lax.rem(z + 7, 8), xl)
    beside = at(y, xh, core, z, 1 - xl)

    barrier = pltpu.get_barrier_semaphore()
    everyone = (up, down, across, other, right, left, beside)
    for device in everyone:
        pl.semaphore_signal(barrier, inc=1, device_id=device, device_id_type=MESH)
    xb[0:T, :] = x_ref[0]
    pl.semaphore_wait(barrier, len(everyone))

    copies = []

    def send(src, dst, device):
        i = len(copies)
        copy = pltpu.make_async_remote_copy(
            src_ref=src, dst_ref=dst, send_sem=ssem.at[i], recv_sem=rsem.at[i],
            device_id=device, device_id_type=MESH,
        )
        copy.start()
        copies.append(copy)
        return copy

    def part(buf, slot, lo, rows, cols):
        return buf.at[pl.ds(SLOT[slot] * T + lo, rows), cols]

    everything = pl.ds(0, N)

    def pass_on(buf, cols, src, dst, device, lo=0, rows=T):
        return send(part(buf, src, lo, rows, cols), part(buf, dst, lo, rows, cols), device)

    cols = everything
    x_up = [pass_on(xb, cols, (0, 0), (3, 0), up, p * H, H) for p in (0, 1)]
    x_down = [pass_on(xb, cols, (0, 0), (1, 0), down, p * H, H) for p in (1, 0)]
    x_across = send(xb.at[pl.ds(0, T), :], xp, across)
    x_other = pass_on(xb, cols, (0, 0), (0, 1), other)
    x_up[0].wait_recv()
    far = [pass_on(xb, cols, (3, 0), (2, 0), up, 0, H)]
    x_down[0].wait_recv()
    far += [pass_on(xb, cols, (1, 0), (2, 0), down, H, H)]
    x_down[1].wait_recv()
    swaps = [pass_on(xb, cols, (1, 0), (1, 1), other)]
    x_up[1].wait_recv()
    swaps += [pass_on(xb, cols, (3, 0), (3, 1), other)]
    x_across.wait_recv()
    x_other.wait_recv()

    def gram(l):
        def chunk(n, carry):
            lo = pl.multiple_of(n * C, C)
            b = xb[pl.ds(l * N + lo, C), :]
            for part_, a_ref in ((0, xb), (1, xp)):
                g = nt(a_ref[0:T, :], b)
                for q in range(4):
                    gp[l, part_ * 4 + q, :, pl.ds(lo, C)] = g[q * S : (q + 1) * S]
            return carry

        lax.fori_loop(0, NC, chunk, 0)

    def share(k):
        return lax.rem(z + k + 16, 8)

    hops = {(0, 0): 4, (0, 1): 3, (1, 0): 3, (1, 1): 4}
    sign = (1, -1)
    to = (right, left)
    base = {(0, 0): 0, (0, 1): 4, (1, 0): 7, (1, 1): 10}
    moving = {}

    def rs_first(l):
        for way in (0, 1):
            h = hops[l, way]
            stage[l * 2 + way] = gp[l, share(sign[way] * h)].astype(jnp.bfloat16)
            moving[l, way, 0] = send(stage.at[l * 2 + way], rs.at[base[l, way]], to[way])

    def rs_step(l, t):
        for way in (0, 1):
            h = hops[l, way]
            if t < h:
                moving[l, way, t - 1].wait_recv()
                slot = base[l, way] + t - 1
                total = rs[slot].astype(jnp.float32) + gp[l, share(sign[way] * (h - t))]
                rs[slot] = total.astype(jnp.bfloat16)
                moving[l, way, t] = send(rs.at[slot], rs.at[slot + 1], to[way])

    def rs_last(l):
        total = gp[l, share(0)]
        for way in (0, 1):
            h = hops[l, way]
            moving[l, way, h - 1].wait_recv()
            total += rs[base[l, way] + h - 1].astype(jnp.float32)
        gp[l, share(0)] = total
        xs[l] = total.astype(jnp.bfloat16)
        moving[l] = send(xs.at[l], xr.at[l], beside)

    def ag_first(l):
        moving[l].wait_recv()
        total = gp[l, share(0)] + xr[l].astype(jnp.float32)
        ga[l, share(0)] = total.astype(jnp.bfloat16)
        for way in (0, 1):
            mine = ga.at[l, share(0)]
            moving[l, way, 0] = send(mine, mine, to[way])

    def ag_step(l, t):
        for way in (0, 1):
            h = hops[l, way]
            if t < h:
                moving[l, way, t - 1].wait_recv()
                block = ga.at[l, share(-sign[way] * t)]
                moving[l, way, t] = send(block, block, to[way])

    def ag_last(l):
        for way in (0, 1):
            moving[l, way, hops[l, way] - 1].wait_recv()
        for m in range(4):
            two = [ga[l, 2 * m + k].astype(jnp.float32) for k in (0, 1)]
            gs[l, m * H : (m + 1) * H, :] = jnp.concatenate(two, 0).astype(jnp.bfloat16)

    swaps[0].wait_recv()
    gram(0)
    rs_first(0)
    for copy in far:
        copy.wait_recv()
    swaps += [pass_on(xb, cols, (2, 0), (2, 1), other)]
    rs_step(0, 1)
    swaps[1].wait_recv()
    swaps[2].wait_recv()
    gram(1)
    rs_first(1)
    rs_step(0, 2)
    rs_step(1, 1)
    rs_step(0, 3)
    rs_step(1, 2)
    rs_last(0)
    rs_step(1, 3)
    ag_first(0)
    rs_last(1)
    ag_step(0, 1)
    ag_first(1)
    ag_step(0, 2)
    ag_step(1, 1)
    ag_step(0, 3)
    ag_step(1, 2)
    ag_last(0)
    ag_step(1, 3)
    ag_last(1)

    def product(buf, lo, cols):
        rows = slice(lo, lo + T)
        out = jnp.dot(gs[0, rows, :], buf[0:N, cols], preferred_element_type=jnp.float32)
        return out + jnp.dot(gs[1, rows, :], buf[N : 2 * N, cols], preferred_element_type=jnp.float32)

    flight = {}

    def stage1(n):
        cols = slice(n * C, (n + 1) * C)
        ys[n] = product(xb, T, cols).astype(jnp.bfloat16)
        flight[1, n] = send(ys.at[n], yr.at[n], across)
        yo[:, cols] = product(xb, 0, cols)

    def stage2(n):
        cols, sl = slice(n * C, (n + 1) * C), pl.ds(n * C, C)
        flight[1, n].wait_recv()
        total = yo[:, cols] + yr[n].astype(jnp.float32)
        yo[:, cols] = total
        vb[0:T, cols] = total.astype(jnp.bfloat16)
        flight[2, n] = (
            pass_on(vb, sl, (0, 0), (3, 0), up),
            pass_on(vb, sl, (0, 0), (1, 0), down),
            pass_on(vb, sl, (0, 0), (0, 1), other),
        )

    def stage3(n):
        sl = pl.ds(n * C, C)
        flight[2, n][0].wait_recv()
        a = pass_on(vb, sl, (3, 0), (2, 0), up, 0, H)
        flight[2, n][1].wait_recv()
        b = pass_on(vb, sl, (1, 0), (2, 0), down, H, H)
        flight[3, n] = (
            a, b,
            pass_on(vb, sl, (3, 0), (3, 1), other),
            pass_on(vb, sl, (1, 0), (1, 1), other),
        )

    def stage4(n):
        sl = pl.ds(n * C, C)
        flight[3, n][0].wait_recv()
        flight[3, n][1].wait_recv()
        flight[4, n] = pass_on(vb, sl, (2, 0), (2, 1), other)

    def stage5(n):
        cols = slice(n * C, (n + 1) * C)
        flight[2, n][2].wait_recv()
        flight[3, n][2].wait_recv()
        flight[3, n][3].wait_recv()
        flight[4, n].wait_recv()
        zs[n] = product(vb, T, cols).astype(jnp.bfloat16)
        flight[5, n] = send(zs.at[n], zr.at[n], across)
        zo[:, cols] = product(vb, 0, cols)

    def stage6(n):
        cols = slice(n * C, (n + 1) * C)
        flight[5, n].wait_recv()
        product_ = coef_cubic * yo[:, cols] + coef_quintic * (zo[:, cols] + zr[n].astype(jnp.float32))
        update = math.sqrt(FFN) * (coef_linear * x_ref[0, :, cols].astype(jnp.float32) + product_)
        update = update.astype(jnp.bfloat16)
        upd_ref[0, :, cols] = update
        new_ref[0, :, cols] = w_ref[0, :, cols] - step_size * update.astype(jnp.float32)

    for step, n in (
        (stage1, 0), (stage1, 1), (stage2, 0), (stage1, 2), (stage2, 1), (stage3, 0), (stage2, 2),
        (stage3, 1), (stage4, 0), (stage3, 2), (stage5, 0), (stage4, 1), (stage5, 1), (stage4, 2),
        (stage6, 0), (stage5, 2), (stage6, 1), (stage6, 2),
    ):
        step(n)

    for copy in copies:
        copy.wait_send()


def per_device(iterate, weights):
    vmem = pl.BlockSpec(memory_space=pltpu.VMEM)
    bf, f32 = jnp.bfloat16, jnp.float32
    return pl.pallas_call(
        kernel,
        out_shape=(
            jax.ShapeDtypeStruct(iterate.shape, bf),
            jax.ShapeDtypeStruct(weights.shape, f32),
        ),
        in_specs=[vmem, vmem],
        out_specs=(vmem, vmem),
        scratch_shapes=[
            pltpu.VMEM((8 * T, N), bf),
            pltpu.VMEM((T, N), bf),
            pltpu.VMEM((2, 8, S, N), f32),
            pltpu.VMEM((4, S, N), bf),
            pltpu.VMEM((14, S, N), bf),
            pltpu.VMEM((2, S, N), bf),
            pltpu.VMEM((2, S, N), bf),
            pltpu.VMEM((2, 8, S, N), bf),
            pltpu.VMEM((2, 2 * T, N), bf),
            pltpu.VMEM((T, N), f32),
            pltpu.VMEM((NC, T, C), bf),
            pltpu.VMEM((NC, T, C), bf),
            pltpu.VMEM((8 * T, N), bf),
            pltpu.VMEM((T, N), f32),
            pltpu.VMEM((NC, T, C), bf),
            pltpu.VMEM((NC, T, C), bf),
            pltpu.SemaphoreType.DMA((N_COPIES,)),
            pltpu.SemaphoreType.DMA((N_COPIES,)),
        ],
        compiler_params=pltpu.CompilerParams(
            collective_id=0, has_side_effects=True, vmem_limit_bytes=56 * 2**20
        ),
        cost_estimate=pl.CostEstimate(flops=9_200_000_000, bytes_accessed=4_000_000, transcendentals=0),
    )(iterate, weights)


def solution(mesh):
    spec = P(None, "row", "col")
    return jax.shard_map(
        per_device, mesh=mesh, in_specs=(spec, spec), out_specs=(spec, spec), check_vma=False
    )
```

time: 527 us -> 143 us (0.27)
  waiting for transfers between devices: 480 us -> 0 us
  Pallas kernels: 0 us -> 139 us
  matrix products: 24 us -> 0 us
  between operations: 13.8 us -> 0.65 us
    all_gather x4 -> x0, waiting for transfers between devices: 325 us -> none  [the longest x1 94.5 us: per_device(): lax.all_gather(own_tile, 'row', axis=0, tiled=True)]
    unnamed x6 -> x0, waiting for transfers between devices: 154 us -> none
    pallas_call x0 -> x1, Pallas kernels: none -> 139 us  [per_device(): pl.pallas_call(kernel, out_shape=(jax.ShapeDtypeStruct(iterate.shape, bf)...]
    dot_general x2 -> x0, matrix products: 13.4 us -> none  [the longest x1 8.72 us: per_device(): jnp.dot(left_part, lax.all_gather(own_tile, 'row', axis=0, tiled=True), p...]
    unnamed x1 -> x0, matrix products: 10.6 us -> none
  transfers between devices with their start and end apart: 5 -> 0, of which waited for: 5 -> 0; matrix products, arithmetic and copies ran while one was open for 0% -> 0% of each run, Pallas kernels for 0% -> 0%
where the time goes in v1:
time: 143 us
  Pallas kernels  139 us (97%)
  local copies, waits for them, and re-layouts  3.15 us (2%)
    pallas_call x1, Pallas kernels, per_device(): pl.pallas_call(kernel, out_shape=(jax.ShapeDtypeStruct(iterate.shape, bf)...  139 us
    unnamed x4, local copies, waits for them, and re-layouts  3.15 us

profile of v1, /device:TPU:1, one launch (start us, length us, event | category | flops | bytes accessed | tf_op | source)
XLA Modules:
  0.0 142.9 jit_solution(262631334977504683)
XLA Ops:
  0.6 139.1 %shard_map.41 = (bf16[1,288,1152]{2,1,0:T(8,128)(2,1)}, f32[1,288,1152]{2,1,0:T(8,128)}) custom-call(bf16[1,288,1152]{2,1,0:T(8,128)(2,1)} %x_ref.1, f32[1,288,1152]{2,1,0:T(8,128)} %w_ref.1), custom_call_target="tpu_custom_call" | custom-call | flops 9200000000 | bytes 4000000 | tf_op jit(solution)/shard_map/pallas_call | solution.py:271
  139.8 0.0 copy-start
  139.8 2.1 %copy.6 = bf16[1,288,1152]{2,1,0:T(8,128)(2,1)} copy(bf16[1,288,1152]{2,1,0:T(8,128)(2,1)} %get-tuple-element.4) | data formatting | bytes 1327104
  141.9 0.0 copy-done
  141.9 1.1 copy.7
Async XLA Ops:
  139.8 2.1 %copy-start = (f32[1,288,1152]{2,1,0:T(8,128)S(1)}, f32[1,288,1152]{2,1,0:T(8,128)}, u32[]{:S(2)}) copy-start(f32[1,288,1152]{2,1,0:T(8,128)} %get-tuple-element.5) | copy-start | bytes 3981316

commit v2 on v0

v2 whole, which is shorter than its diff:
```python
import functools
import math

import jax
import jax.numpy as jnp
from jax import lax
from jax.experimental import pallas as pl
from jax.experimental.pallas import tpu as pltpu
from jax.sharding import PartitionSpec as P

MESH = pl.DeviceIdType.MESH

FFN = 18432
coef_linear = 3.4445
coef_cubic = -4.775
coef_quintic = 2.0315
step_size = 0.02

T = 288
H = 144
N = 1152
K = 8 * T
S = 72
UNITS = ((0, 0, 512), (1, 0, 768), (1, 768, 768), (1, 1536, 768), (0, 512, 512), (0, 1024, 512), (0, 1536, 768))
CHUNKS = (128, 256, 256, 256, 256)
N_COPIES = 192

SLOT = {(0, 0): 0, (0, 1): 1, (1, 0): 2, (1, 1): 3, (3, 0): 4, (3, 1): 5, (2, 0): 6, (2, 1): 7}

HOPS = (4, 3)

ORDER = (
    ("x_own",), ("x_have", "o"), ("gram", 0), ("rs_first", 0), ("rs_step", 0, 1), ("x_far_up",),
    ("x_far_down",), ("rs_step", 0, 2), ("rs_step", 0, 3), ("x_swap", 3), ("x_swap", 1), ("x_have", "x"),
    ("rs_last", 0), ("x_have", 3), ("x_have", 1), ("gram", 2), ("rs_first", 2), ("ag_first", 0), ("x_swap", 2),
    ("gram", 1), ("rs_first", 1), ("gram", 4), ("gram", 5), ("rs_first", 5), ("rs_step", 2, 1), ("x_have", 2),
    ("gram", 3), ("rs_first", 3), ("ag_step", 0, 1), ("rs_step", 1, 1), ("gram", 6), ("rs_first", 6),
    ("rs_step", 5, 1), ("rs_step", 2, 2), ("rs_step", 3, 1), ("ag_step", 0, 2), ("rs_step", 1, 2),
    ("rs_first", 4), ("rs_step", 2, 3), ("rs_step", 6, 1), ("rs_step", 5, 2), ("rs_step", 1, 3),
    ("rs_step", 3, 2), ("rs_last", 2), ("ag_step", 0, 3), ("rs_step", 5, 3), ("rs_step", 4, 1), ("rs_last", 1),
    ("rs_step", 3, 3), ("rs_step", 6, 2), ("ag_first", 2), ("ag_step", 0, 4), ("assemble", 0), ("rs_last", 5),
    ("ag_first", 1), ("rs_step", 4, 2), ("rs_last", 3), ("rs_step", 6, 3), ("ag_step", 2, 1),
    ("ag_step", 1, 1), ("rs_step", 4, 3), ("ag_first", 3), ("rs_last", 6), ("ag_step", 2, 2),
    ("ag_step", 1, 2), ("ag_first", 5), ("rs_last", 4), ("ag_first", 6), ("ag_step", 3, 1), ("ag_step", 2, 3),
    ("ag_step", 1, 3), ("ag_first", 4), ("ag_step", 5, 1), ("ag_step", 6, 1), ("ag_step", 2, 4),
    ("assemble", 2), ("ag_step", 3, 2), ("ag_step", 1, 4), ("assemble", 1), ("ag_step", 4, 1),
    ("ag_step", 5, 2), ("ag_step", 6, 2), ("ag_step", 3, 3), ("ag_step", 4, 2), ("ag_step", 5, 3),
    ("ag_step", 6, 3), ("ag_step", 3, 4), ("assemble", 3), ("y_partner", 0), ("y_partner", 1),
    ("ag_step", 4, 3), ("y_partner", 2), ("ag_step", 5, 4), ("assemble", 5), ("y_partner", 3),
    ("ag_step", 6, 4), ("assemble", 6), ("y_partner", 4), ("ag_step", 4, 4), ("assemble", 4), ("y_own", 0),
    ("v_own", 0), ("y_own", 1), ("y_own", 2), ("y_own", 3), ("v_own", 1), ("y_own", 4), ("v_up", 0),
    ("v_down", 0), ("v_own", 2), ("v_up", 1), ("v_down", 1), ("v_own", 3), ("v_far", 0), ("z_both", 0),
    ("v_up", 2), ("v_down", 2), ("v_own", 4), ("v_far", 1), ("z_both", 1), ("finish", 0), ("v_down", 3),
    ("v_up", 3), ("v_far", 2), ("z_both", 2), ("v_down", 4), ("v_up", 4), ("finish", 1), ("v_far", 3),
    ("z_both", 3), ("v_far", 4), ("finish", 2), ("z_both", 4), ("finish", 3), ("finish", 4),
)


def nt(a, b):
    return lax.dot_general(a, b, (((1,), (1,)), ((), ())), preferred_element_type=jnp.float32)


def kernel(
    x_ref, out_ref,
    xb, xp, gp, stage, rs, xs, xr, ga, gs, yo, ys, yr, vb, zo, zs, zr, ssem, rsem, own_sem,
):
    r, c = lax.axis_index("row"), lax.axis_index("col")
    core, xh, y = lax.rem(r, 2), lax.rem(r // 2, 2), r // 4
    xl, z = lax.rem(c, 2), c // 2
    turn = 1 - 2 * core

    def at(y_, xh_, core_, z_, xl_):
        return ((y_ * 2 + xh_) * 2 + core_, z_ * 2 + xl_)

    up = at(lax.rem(y + 1, 4), xh, core, z, xl)
    down = at(lax.rem(y + 3, 4), xh, core, z, xl)
    across = at(y, 1 - xh, core, z, xl)
    other = at(y, xh, 1 - core, z, xl)
    ways = (
        at(y, xh, core, lax.rem(z + turn + 8, 8), xl),
        at(y, xh, core, lax.rem(z - turn + 8, 8), xl),
    )
    beside = at(y, xh, core, z, 1 - xl)

    barrier = pltpu.get_barrier_semaphore()
    everyone = (up, down, across, other, *ways, beside)
    for device in everyone:
        pl.semaphore_signal(barrier, inc=1, device_id=device, device_id_type=MESH)
    own = pltpu.make_async_copy(x_ref.at[0], xb.at[pl.ds(0, T), :], own_sem)
    own.start()
    pl.semaphore_wait(barrier, len(everyone))
    own.wait()

    copies = []
    flight = {}

    def send(src, dst, device):
        i = len(copies)
        copy = pltpu.make_async_remote_copy(
            src_ref=src, dst_ref=dst, send_sem=ssem.at[i], recv_sem=rsem.at[i],
            device_id=device, device_id_type=MESH,
        )
        copy.start()
        copies.append(copy)
        return copy

    def arrive(*key):
        flight[key].wait_recv()

    def part(buf, slot, lo, rows, cols):
        return buf.at[pl.ds(SLOT[slot] * T + lo, rows), cols]

    def pass_on(buf, cols, src, dst, device, lo=0, rows=T):
        return send(part(buf, src, lo, rows, cols), part(buf, dst, lo, rows, cols), device)

    every = pl.ds(0, N)

    def x_own():
        for p in (0, 1):
            flight["xu", p] = pass_on(xb, every, (0, 0), (3, 0), up, p * H, H)
            flight["xd", 1 - p] = pass_on(xb, every, (0, 0), (1, 0), down, (1 - p) * H, H)
            if p == 0:
                flight["xo"] = pass_on(xb, every, (0, 0), (0, 1), other)
        flight["xx"] = send(xb.at[pl.ds(0, T), :], xp, across)

    def x_far_up():
        arrive("xu", 0)
        flight["xfu"] = pass_on(xb, every, (3, 0), (2, 0), up, 0, H)

    def x_far_down():
        arrive("xd", 1)
        flight["xfd"] = pass_on(xb, every, (1, 0), (2, 0), down, H, H)

    def x_swap(dy):
        if dy == 1:
            arrive("xd", 0)
        elif dy == 3:
            arrive("xu", 1)
        else:
            flight["xfu"].wait_recv()
            flight["xfd"].wait_recv()
        flight["xs", dy] = pass_on(xb, every, (dy, 0), (dy, 1), other)

    def x_have(what):
        if what == "x":
            flight["xx"].wait_recv()
        elif what == "o":
            flight["xo"].wait_recv()
        else:
            arrive("xs", what)

    def gram(n):
        a, lo, w = UNITS[n]
        g = nt((xb, xp)[a][0:T, :], xb[lo : lo + w, :])
        for q in range(4):
            for m in range(2):
                gp[n][q * 2 + m] = g[q * S : (q + 1) * S, m * (w // 2) : (m + 1) * (w // 2)]

    def share(k):
        return lax.rem(z + turn * k + 16, 8)

    def rs_first(n):
        for way, h in enumerate(HOPS):
            stage[n][way] = gp[n][share((h, -h)[way])].astype(jnp.bfloat16)
            flight["r", n, way, 0] = send(stage[n].at[way], rs[n].at[way * 4], ways[way])

    def rs_step(n, t):
        for way, h in enumerate(HOPS):
            if t < h:
                arrive("r", n, way, t - 1)
                slot, k = way * 4 + t - 1, (h - t, t - h)[way]
                total = rs[n][slot].astype(jnp.float32) + gp[n][share(k)]
                rs[n][slot] = total.astype(jnp.bfloat16)
                flight["r", n, way, t] = send(rs[n].at[slot], rs[n].at[slot + 1], ways[way])

    def rs_last(n):
        total = gp[n][share(0)]
        for way, h in enumerate(HOPS):
            arrive("r", n, way, h - 1)
            total += rs[n][way * 4 + h - 1].astype(jnp.float32)
        gp[n][share(0)] = total
        xs[n][...] = total.astype(jnp.bfloat16)
        flight["x", n] = send(xs[n], xr[n], beside)

    def ag_send(n, way, t):
        block = ga[n].at[share((-t, t)[way])]
        flight["g", n, way, t] = send(block, block, ways[way])

    def ag_first(n):
        arrive("x", n)
        total = gp[n][share(0)] + xr[n][...].astype(jnp.float32)
        ga[n][share(0)] = total.astype(jnp.bfloat16)
        for way in (0, 1):
            ag_send(n, way, 0)

    def ag_step(n, t):
        for way, h in enumerate(HOPS):
            if t <= h:
                arrive("g", n, way, t - 1)
                if t < h:
                    ag_send(n, way, t)

    def assemble(n):
        a, lo, w = UNITS[n]
        for m in range(2):
            rows = [ga[n][q * 2 + m].astype(jnp.float32) for q in range(4)]
            cols = slice(lo + m * (w // 2), lo + (m + 1) * (w // 2))
            gs[a * T : (a + 1) * T, cols] = jnp.concatenate(rows, 0).astype(jnp.bfloat16)

    def cols_of(n):
        lo = sum(CHUNKS[:n])
        return slice(lo, lo + CHUNKS[n]), pl.ds(lo, CHUNKS[n])

    def product(rows, buf, cols):
        return jnp.dot(gs[rows, :], buf[:, cols], preferred_element_type=jnp.float32)

    def y_partner(n):
        cols, sl = cols_of(n)
        ys[:, cols] = product(slice(T, 2 * T), xb, cols).astype(jnp.bfloat16)
        flight["y", n] = send(ys.at[:, sl], yr.at[:, sl], across)

    def y_own(n):
        cols, _ = cols_of(n)
        yo[:, cols] = product(slice(0, T), xb, cols)

    def v_own(n):
        cols, sl = cols_of(n)
        arrive("y", n)
        total = yo[:, cols] + yr[:, cols].astype(jnp.float32)
        yo[:, cols] = total
        vb[0:T, cols] = total.astype(jnp.bfloat16)
        flight["vu", n] = pass_on(vb, sl, (0, 0), (3, 0), up)
        flight["vd", n] = pass_on(vb, sl, (0, 0), (1, 0), down)
        flight["vo", n] = pass_on(vb, sl, (0, 0), (0, 1), other)

    def v_up(n):
        _, sl = cols_of(n)
        arrive("vu", n)
        flight["vfu", n] = pass_on(vb, sl, (3, 0), (2, 0), up, 0, H)
        flight["vs", 3, n] = pass_on(vb, sl, (3, 0), (3, 1), other)

    def v_down(n):
        _, sl = cols_of(n)
        arrive("vd", n)
        flight["vfd", n] = pass_on(vb, sl, (1, 0), (2, 0), down, H, H)
        flight["vs", 1, n] = pass_on(vb, sl, (1, 0), (1, 1), other)

    def v_far(n):
        _, sl = cols_of(n)
        arrive("vfu", n)
        arrive("vfd", n)
        flight["vs", 2, n] = pass_on(vb, sl, (2, 0), (2, 1), other)

    def z_both(n):
        cols, sl = cols_of(n)
        arrive("vo", n)
        for dy in (1, 3, 2):
            arrive("vs", dy, n)
        both = product(slice(0, 2 * T), vb, cols)
        zs[:, cols] = both[T:].astype(jnp.bfloat16)
        flight["z", n] = send(zs.at[:, sl], zr.at[:, sl], across)
        zo[:, cols] = both[:T]

    def finish(n):
        cols, _ = cols_of(n)
        arrive("z", n)
        product_ = coef_cubic * yo[:, cols] + coef_quintic * (zo[:, cols] + zr[:, cols].astype(jnp.float32))
        out_ref[0, :, cols] = math.sqrt(FFN) * (coef_linear * xb[0:T, cols].astype(jnp.float32) + product_)

    steps = (
        x_own, x_far_up, x_far_down, x_swap, x_have, gram, rs_first, rs_step, rs_last,
        ag_first, ag_step, assemble, y_partner, y_own, v_own, v_up, v_down, v_far, z_both, finish,
    )
    steps = {step.__name__: step for step in steps}
    for name, *args in ORDER:
        steps[name](*args)

    for copy in copies:
        copy.wait_send()


def per_device(iterate, weights):
    vmem = pl.BlockSpec(memory_space=pltpu.VMEM)
    bf, f32 = jnp.bfloat16, jnp.float32

    def per_unit(dtype, *shape):
        return [pltpu.VMEM((*shape, w // 2), dtype) for _, _, w in UNITS]

    scaled = pl.pallas_call(
        kernel,
        out_shape=jax.ShapeDtypeStruct(weights.shape, f32),
        in_specs=[pl.BlockSpec(memory_space=pltpu.HBM)],
        out_specs=vmem,
        scratch_shapes=[
            pltpu.VMEM((K, N), bf),
            pltpu.VMEM((T, N), bf),
            per_unit(f32, 8, S),
            per_unit(bf, 2, S),
            per_unit(bf, 7, S),
            per_unit(bf, S),
            per_unit(bf, S),
            per_unit(bf, 8, S),
            pltpu.VMEM((2 * T, K), bf),
            pltpu.VMEM((T, N), f32),
            pltpu.VMEM((T, N), bf),
            pltpu.VMEM((T, N), bf),
            pltpu.VMEM((K, N), bf),
            pltpu.VMEM((T, N), f32),
            pltpu.VMEM((T, N), bf),
            pltpu.VMEM((T, N), bf),
            pltpu.SemaphoreType.DMA((N_COPIES,)),
            pltpu.SemaphoreType.DMA((N_COPIES,)),
            pltpu.SemaphoreType.DMA,
        ],
        compiler_params=pltpu.CompilerParams(
            collective_id=0, has_side_effects=True, vmem_limit_bytes=40 * 2**20
        ),
        cost_estimate=pl.CostEstimate(flops=9_200_000_000, bytes_accessed=4_000_000, transcendentals=0),
    )(iterate)
    update = scaled.astype(bf)
    return update, weights - step_size * update.astype(f32)


def solution(mesh):
    spec = P(None, "row", "col")
    return jax.shard_map(
        per_device, mesh=mesh, in_specs=(spec, spec), out_specs=(spec, spec), check_vma=False
    )
```

time: 527 us -> 126 us (0.24)
  waiting for transfers between devices: 480 us -> 0 us
  Pallas kernels: 0 us -> 123 us
  matrix products: 24 us -> 0 us
  between operations: 13.8 us -> 0.65 us
    all_gather x4 -> x0, waiting for transfers between devices: 325 us -> none  [the longest x1 94.5 us: per_device(): lax.all_gather(own_tile, 'row', axis=0, tiled=True)]
    unnamed x6 -> x0, waiting for transfers between devices: 154 us -> none
    pallas_call x0 -> x1, Pallas kernels: none -> 123 us  [per_device(): pl.pallas_call(kernel, out_shape=jax.ShapeDtypeStruct(weights.shape, f32)...]
    dot_general x2 -> x0, matrix products: 13.4 us -> none  [the longest x1 8.72 us: per_device(): jnp.dot(left_part, lax.all_gather(own_tile, 'row', axis=0, tiled=True), p...]
    unnamed x1 -> x0, matrix products: 10.6 us -> none
  transfers between devices with their start and end apart: 5 -> 0, of which waited for: 5 -> 0; matrix products, arithmetic and copies ran while one was open for 0% -> 0% of each run, Pallas kernels for 0% -> 0%
where the time goes in v2:
time: 126 us
  Pallas kernels  123 us (98%)
  other arithmetic  1.45 us (1%)
    pallas_call x1, Pallas kernels, per_device(): pl.pallas_call(kernel, out_shape=jax.ShapeDtypeStruct(weights.shape, f32)...  123 us

profile of v2, /device:TPU:1, one launch (start us, length us, event | category | flops | bytes accessed | tf_op | source)
XLA Modules:
  0.0 125.8 jit_solution(14121485166375509604)
XLA Ops:
  0.6 0.0 copy-start
  0.6 1.1 copy-done
  1.7 0.0 copy-start.1
  1.7 122.6 %shard_map.41 = f32[1,288,1152]{2,1,0:T(8,128)S(1)} custom-call(bf16[1,288,1152]{2,1,0:T(8,128)(2,1)S(1)} %copy-done), custom_call_target="tpu_custom_call" | custom-call | flops 9200000000 | bytes 4000000 | tf_op jit(solution)/shard_map/pallas_call | solution.py:289
  124.3 0.0 copy-done.1
  124.4 1.4 %multiply_subtract_fusion = (f32[1,288,1152]{2,1,0:T(8,128)}, bf16[1,288,1152]{2,1,0:T(8,128)(2,1)}) fusion(f32[1,288,1152]{2,1,0:T(8,128)S(1)} %copy-done.1, f32[1,288,1152]{2,1,0:T(8,128)S(1)} %shard_map.41), kind=kLoop, calls=%fused_computation | loop fusion | flops 1327104 | bytes 4644864 | tf_op jit(solution)/shard_map/sub | solution.py:321
Async XLA Ops:
  0.6 1.1 copy-start
  1.7 122.6 %copy-start.1 = (f32[1,288,1152]{2,1,0:T(8,128)S(1)}, f32[1,288,1152]{2,1,0:T(8,128)}, u32[]{:S(2)}) copy-start(f32[1,288,1152]{2,1,0:T(8,128)} %param.3) | copy-start | bytes 3981316

commit v3 on v2

--- a/solution.py
+++ b/solution.py
@@ -21,38 +21,53 @@
 N = 1152
 K = 8 * T
 S = 72
-UNITS = ((0, 0, 512), (1, 0, 768), (1, 768, 768), (1, 1536, 768), (0, 512, 512), (0, 1024, 512), (0, 1536, 768))
+PLACE = {
+    (0, 0, 0): 0, (0, 0, 1): 144, (0, 1, 0): 288, (0, 1, 1): 432,
+    (3, 0, 0): 576, (3, 1, 0): 720, (1, 0, 1): 864, (1, 1, 1): 1008,
+    (3, 0, 1): 1152, (3, 1, 1): 1296, (1, 0, 0): 1440, (1, 1, 0): 1584,
+    (2, 0, 0): 1728, (2, 1, 0): 1872, (2, 0, 1): 2016, (2, 1, 1): 2160,
+}
+
+UNITS = ((0, 0, 512), (0, 512, 512), (0, 1024, 512), (1, 0, 512), (1, 512, 512), (1, 1024, 512), (1, 1536, 512), (1, 2048, 256), (0, 1536, 512), (0, 2048, 256))
 CHUNKS = (128, 256, 256, 256, 256)
-N_COPIES = 192
-
-SLOT = {(0, 0): 0, (0, 1): 1, (1, 0): 2, (1, 1): 3, (3, 0): 4, (3, 1): 5, (2, 0): 6, (2, 1): 7}
+N_COPIES = 256
 
 HOPS = (4, 3)
 
+(
+    X_OWN, X_UP, X_DOWN, X_FAR, X_HAVE, GRAM, RS_FIRST, RS_STEP, RS_LAST, AG_FIRST, AG_STEP, ASSEMBLE,
+    Y_PARTNER, Y_OWN, V_OWN, V_UP, V_DOWN, V_FAR, Z_BOTH, FINISH,
+) = range(20)
 ORDER = (
-    ("x_own",), ("x_have", "o"), ("gram", 0), ("rs_first", 0), ("rs_step", 0, 1), ("x_far_up",),
-    ("x_far_down",), ("rs_step", 0, 2), ("rs_step", 0, 3), ("x_swap", 3), ("x_swap", 1), ("x_have", "x"),
-    ("rs_last", 0), ("x_have", 3), ("x_have", 1), ("gram", 2), ("rs_first", 2), ("ag_first", 0), ("x_swap", 2),
-    ("gram", 1), ("rs_first", 1), ("gram", 4), ("gram", 5), ("rs_first", 5), ("rs_step", 2, 1), ("x_have", 2),
-    ("gram", 3), ("rs_first", 3), ("ag_step", 0, 1), ("rs_step", 1, 1), ("gram", 6), ("rs_first", 6),
-    ("rs_step", 5, 1), ("rs_step", 2, 2), ("rs_step", 3, 1), ("ag_step", 0, 2), ("rs_step", 1, 2),
-    ("rs_first", 4), ("rs_step", 2, 3), ("rs_step", 6, 1), ("rs_step", 5, 2), ("rs_step", 1, 3),
-    ("rs_step", 3, 2), ("rs_last", 2), ("ag_step", 0, 3), ("rs_step", 5, 3), ("rs_step", 4, 1), ("rs_last", 1),
-    ("rs_step", 3, 3), ("rs_step", 6, 2), ("ag_first", 2), ("ag_step", 0, 4), ("assemble", 0), ("rs_last", 5),
-    ("ag_first", 1), ("rs_step", 4, 2), ("rs_last", 3), ("rs_step", 6, 3), ("ag_step", 2, 1),
-    ("ag_step", 1, 1), ("rs_step", 4, 3), ("ag_first", 3), ("rs_last", 6), ("ag_step", 2, 2),
-    ("ag_step", 1, 2), ("ag_first", 5), ("rs_last", 4), ("ag_first", 6), ("ag_step", 3, 1), ("ag_step", 2, 3),
-    ("ag_step", 1, 3), ("ag_first", 4), ("ag_step", 5, 1), ("ag_step", 6, 1), ("ag_step", 2, 4),
-    ("assemble", 2), ("ag_step", 3, 2), ("ag_step", 1, 4), ("assemble", 1), ("ag_step", 4, 1),
-    ("ag_step", 5, 2), ("ag_step", 6, 2), ("ag_step", 3, 3), ("ag_step", 4, 2), ("ag_step", 5, 3),
-    ("ag_step", 6, 3), ("ag_step", 3, 4), ("assemble", 3), ("y_partner", 0), ("y_partner", 1),
-    ("ag_step", 4, 3), ("y_partner", 2), ("ag_step", 5, 4), ("assemble", 5), ("y_partner", 3),
-    ("ag_step", 6, 4), ("assemble", 6), ("y_partner", 4), ("ag_step", 4, 4), ("assemble", 4), ("y_own", 0),
-    ("v_own", 0), ("y_own", 1), ("y_own", 2), ("y_own", 3), ("v_own", 1), ("y_own", 4), ("v_up", 0),
-    ("v_down", 0), ("v_own", 2), ("v_up", 1), ("v_down", 1), ("v_own", 3), ("v_far", 0), ("z_both", 0),
-    ("v_up", 2), ("v_down", 2), ("v_own", 4), ("v_far", 1), ("z_both", 1), ("finish", 0), ("v_down", 3),
-    ("v_up", 3), ("v_far", 2), ("z_both", 2), ("v_down", 4), ("v_up", 4), ("finish", 1), ("v_far", 3),
-    ("z_both", 3), ("v_far", 4), ("finish", 2), ("z_both", 4), ("finish", 3), ("finish", 4),
+    (X_OWN,), (X_HAVE, 0), (GRAM, 0), (RS_FIRST, 0), (RS_STEP, 0, 1), (X_UP, 0), (X_DOWN, 1), (RS_STEP, 0, 2),
+    (X_HAVE, 2), (GRAM, 1), (RS_FIRST, 1), (RS_STEP, 0, 3), (X_UP, 1), (X_DOWN, 0), (X_HAVE, 1),
+    (RS_STEP, 1, 1), (GRAM, 3), (RS_FIRST, 3), (RS_LAST, 0), (GRAM, 4), (RS_FIRST, 4), (X_HAVE, 3), (GRAM, 5),
+    (RS_FIRST, 5), (RS_STEP, 1, 2), (GRAM, 2), (X_FAR, 0), (RS_STEP, 3, 1), (RS_FIRST, 2), (X_FAR, 1),
+    (RS_STEP, 4, 1), (RS_STEP, 5, 1), (RS_STEP, 1, 3), (X_HAVE, 4), (GRAM, 7), (RS_FIRST, 7), (RS_STEP, 3, 2),
+    (GRAM, 6), (RS_FIRST, 6), (RS_STEP, 2, 1), (RS_STEP, 4, 2), (RS_LAST, 1), (GRAM, 8), (RS_STEP, 7, 1),
+    (RS_STEP, 5, 2), (RS_STEP, 3, 3), (RS_FIRST, 8), (GRAM, 9), (RS_FIRST, 9), (RS_STEP, 6, 1),
+    (RS_STEP, 4, 3), (RS_STEP, 2, 2), (RS_STEP, 5, 3), (AG_FIRST, 0), (RS_STEP, 7, 2), (RS_LAST, 3),
+    (RS_STEP, 8, 1), (RS_STEP, 9, 1), (RS_LAST, 4), (RS_STEP, 6, 2), (RS_STEP, 2, 3), (AG_FIRST, 3),
+    (RS_LAST, 5), (RS_STEP, 7, 3), (AG_STEP, 0, 1), (AG_FIRST, 4), (RS_STEP, 8, 2), (RS_STEP, 6, 3),
+    (RS_STEP, 9, 2), (RS_LAST, 2), (RS_LAST, 7), (AG_STEP, 3, 1), (AG_STEP, 0, 2), (RS_STEP, 8, 3),
+    (AG_STEP, 4, 1), (RS_LAST, 6), (AG_FIRST, 7), (AG_FIRST, 5), (RS_STEP, 9, 3), (AG_STEP, 3, 2),
+    (RS_LAST, 8), (AG_STEP, 0, 3), (AG_FIRST, 6), (AG_STEP, 4, 2), (AG_STEP, 7, 1), (RS_LAST, 9),
+    (AG_STEP, 5, 1), (AG_FIRST, 8), (AG_STEP, 0, 4), (ASSEMBLE, 0), (AG_STEP, 3, 3), (AG_STEP, 6, 1),
+    (AG_FIRST, 9), (AG_STEP, 4, 3), (AG_STEP, 7, 2), (AG_STEP, 5, 2), (AG_FIRST, 2), (AG_FIRST, 1),
+    (AG_STEP, 3, 4), (AG_STEP, 8, 1), (ASSEMBLE, 3), (AG_STEP, 6, 2), (AG_STEP, 9, 1), (AG_STEP, 4, 4),
+    (ASSEMBLE, 4), (AG_STEP, 7, 3), (AG_STEP, 5, 3), (AG_STEP, 2, 1), (AG_STEP, 1, 1), (AG_STEP, 8, 2),
+    (AG_STEP, 7, 4), (ASSEMBLE, 7), (AG_STEP, 6, 3), (AG_STEP, 5, 4), (ASSEMBLE, 5), (AG_STEP, 9, 2),
+    (AG_STEP, 2, 2), (AG_STEP, 1, 2), (AG_STEP, 6, 4), (ASSEMBLE, 6), (AG_STEP, 8, 3), (Y_PARTNER, 0),
+    (Y_PARTNER, 1), (AG_STEP, 9, 3), (AG_STEP, 2, 3), (Y_PARTNER, 2), (AG_STEP, 1, 3), (Y_PARTNER, 3),
+    (AG_STEP, 8, 4), (ASSEMBLE, 8), (Y_PARTNER, 4), (AG_STEP, 9, 4), (ASSEMBLE, 9), (AG_STEP, 2, 4),
+    (ASSEMBLE, 2), (AG_STEP, 1, 4), (ASSEMBLE, 1), (Y_OWN, 0), (V_OWN, 0), (Y_OWN, 1), (V_OWN, 1), (Y_OWN, 2),
+    (Y_OWN, 3), (Y_OWN, 4), (V_UP, 0, 0), (V_UP, 1, 0), (V_DOWN, 1, 0), (V_DOWN, 0, 0), (V_OWN, 2),
+    (V_UP, 0, 1), (V_DOWN, 1, 1), (V_UP, 1, 1), (V_DOWN, 0, 1), (V_OWN, 3), (V_FAR, 0, 0), (V_FAR, 1, 0),
+    (V_UP, 0, 2), (V_DOWN, 1, 2), (Z_BOTH, 0), (V_DOWN, 0, 2), (V_OWN, 4), (V_UP, 1, 2), (V_FAR, 0, 1),
+    (V_FAR, 1, 1), (V_UP, 0, 3), (V_DOWN, 1, 3), (Z_BOTH, 1), (V_DOWN, 0, 3), (V_UP, 1, 3), (FINISH, 0),
+    (V_FAR, 0, 2), (V_FAR, 1, 2), (V_UP, 0, 4), (V_DOWN, 1, 4), (Z_BOTH, 2), (V_DOWN, 0, 4), (V_UP, 1, 4),
+    (V_FAR, 0, 3), (V_FAR, 1, 3), (FINISH, 1), (V_FAR, 0, 4), (V_FAR, 1, 4), (Z_BOTH, 3), (Z_BOTH, 4),
+    (FINISH, 2), (FINISH, 3), (FINISH, 4),
 )
 
 
@@ -107,47 +122,52 @@
     def arrive(*key):
         flight[key].wait_recv()
 
-    def part(buf, slot, lo, rows, cols):
-        return buf.at[pl.ds(SLOT[slot] * T + lo, rows), cols]
-
-    def pass_on(buf, cols, src, dst, device, lo=0, rows=T):
-        return send(part(buf, src, lo, rows, cols), part(buf, dst, lo, rows, cols), device)
+    def half(buf, dy, swapped, p, cols):
+        return buf.at[pl.ds(PLACE[dy, swapped, p], H), cols]
+
+    def pass_up(buf, dy, p, cols):
+        return send(half(buf, dy, 0, p, cols), half(buf, (dy + 3) % 4, 0, p, cols), up)
+
+    def pass_down(buf, dy, p, cols):
+        return send(half(buf, dy, 0, p, cols), half(buf, (dy + 1) % 4, 0, p, cols), down)
+
+    def swap(buf, dy, p, cols):
+        return send(half(buf, dy, 0, p, cols), half(buf, dy, 1, p, cols), other)
 
     every = pl.ds(0, N)
 
     def x_own():
-        for p in (0, 1):
-            flight["xu", p] = pass_on(xb, every, (0, 0), (3, 0), up, p * H, H)
-            flight["xd", 1 - p] = pass_on(xb, every, (0, 0), (1, 0), down, (1 - p) * H, H)
-            if p == 0:
-                flight["xo"] = pass_on(xb, every, (0, 0), (0, 1), other)
-        flight["xx"] = send(xb.at[pl.ds(0, T), :], xp, across)
-
-    def x_far_up():
-        arrive("xu", 0)
-        flight["xfu"] = pass_on(xb, every, (3, 0), (2, 0), up, 0, H)
-
-    def x_far_down():
-        arrive("xd", 1)
-        flight["xfd"] = pass_on(xb, every, (1, 0), (2, 0), down, H, H)
-
-    def x_swap(dy):
-        if dy == 1:
-            arrive("xd", 0)
-        elif dy == 3:
-            arrive("xu", 1)
+        flight["xu", 0] = pass_up(xb, 0, 0, every)
+        flight["xd", 1] = pass_down(xb, 0, 1, every)
+        flight["xo",] = send(xb.at[pl.ds(0, T), :], xb.at[pl.ds(T, T), :], other)
+        flight["xu", 1] = pass_up(xb, 0, 1, every)
+        flight["xd", 0] = pass_down(xb, 0, 0, every)
+        flight["xx",] = send(xb.at[pl.ds(0, T), :], xp, across)
+
+    def x_up(p):
+        arrive("xu", p)
+        if p == 0:
+            flight["xf", 0] = pass_up(xb, 3, 0, every)
+        flight["xs", 3, p] = swap(xb, 3, p, every)
+
+    def x_down(p):
+        arrive("xd", p)
+        if p == 1:
+            flight["xf", 1] = pass_down(xb, 1, 1, every)
+        flight["xs", 1, p] = swap(xb, 1, p, every)
+
+    def x_far(p):
+        arrive("xf", p)
+        flight["xs", 2, p] = swap(xb, 2, p, every)
+
+    def x_have(what):
+        if what == 0:
+            arrive("xo")
+        elif what == 1:
+            arrive("xx")
         else:
-            flight["xfu"].wait_recv()
-            flight["xfd"].wait_recv()
-        flight["xs", dy] = pass_on(xb, every, (dy, 0), (dy, 1), other)
-
-    def x_have(what):
-        if what == "x":
-            flight["xx"].wait_recv()
-        elif what == "o":
-            flight["xo"].wait_recv()
-        else:
-            arrive("xs", what)
+            for dy, p in (((3, 0), (1, 1)), ((3, 1), (1, 0)), ((2, 0), (2, 1)))[what - 2]:
+                arrive("xs", dy, p)
 
     def gram(n):
         a, lo, w = UNITS[n]
@@ -229,33 +249,37 @@
         total = yo[:, cols] + yr[:, cols].astype(jnp.float32)
         yo[:, cols] = total
         vb[0:T, cols] = total.astype(jnp.bfloat16)
-        flight["vu", n] = pass_on(vb, sl, (0, 0), (3, 0), up)
-        flight["vd", n] = pass_on(vb, sl, (0, 0), (1, 0), down)
-        flight["vo", n] = pass_on(vb, sl, (0, 0), (0, 1), other)
-
-    def v_up(n):
+        flight["vu", 0, n] = pass_up(vb, 0, 0, sl)
+        flight["vd", 1, n] = pass_down(vb, 0, 1, sl)
+        flight["vo", n] = send(vb.at[pl.ds(0, T), sl], vb.at[pl.ds(T, T), sl], other)
+        flight["vu", 1, n] = pass_up(vb, 0, 1, sl)
+        flight["vd", 0, n] = pass_down(vb, 0, 0, sl)
+
+    def v_up(p, n):
         _, sl = cols_of(n)
-        arrive("vu", n)
-        flight["vfu", n] = pass_on(vb, sl, (3, 0), (2, 0), up, 0, H)
-        flight["vs", 3, n] = pass_on(vb, sl, (3, 0), (3, 1), other)
-
-    def v_down(n):
+        arrive("vu", p, n)
+        if p == 0:
+            flight["vf", 0, n] = pass_up(vb, 3, 0, sl)
+        flight["vs", 3, p, n] = swap(vb, 3, p, sl)
+
+    def v_down(p, n):
         _, sl = cols_of(n)
-        arrive("vd", n)
-        flight["vfd", n] = pass_on(vb, sl, (1, 0), (2, 0), down, H, H)
-        flight["vs", 1, n] = pass_on(vb, sl, (1, 0), (1, 1), other)
-
-    def v_far(n):
+        arrive("vd", p, n)
+        if p == 1:
+            flight["vf", 1, n] = pass_down(vb, 1, 1, sl)
+        flight["vs", 1, p, n] = swap(vb, 1, p, sl)
+
+    def v_far(p, n):
         _, sl = cols_of(n)
-        arrive("vfu", n)
-        arrive("vfd", n)
-        flight["vs", 2, n] = pass_on(vb, sl, (2, 0), (2, 1), other)
+        arrive("vf", p, n)
+        flight["vs", 2, p, n] = swap(vb, 2, p, sl)
 
     def z_both(n):
         cols, sl = cols_of(n)
         arrive("vo", n)
         for dy in (1, 3, 2):
-            arrive("vs", dy, n)
+            for p in (0, 1):
+                arrive("vs", dy, p, n)
         both = product(slice(0, 2 * T), vb, cols)
         zs[:, cols] = both[T:].astype(jnp.bfloat16)
         flight["z", n] = send(zs.at[:, sl], zr.at[:, sl], across)
@@ -268,12 +292,11 @@
         out_ref[0, :, cols] = math.sqrt(FFN) * (coef_linear * xb[0:T, cols].astype(jnp.float32) + product_)
 
     steps = (
-        x_own, x_far_up, x_far_down, x_swap, x_have, gram, rs_first, rs_step, rs_last,
+        x_own, x_up, x_down, x_far, x_have, gram, rs_first, rs_step, rs_last,
         ag_first, ag_step, assemble, y_partner, y_own, v_own, v_up, v_down, v_far, z_both, finish,
     )
-    steps = {step.__name__: step for step in steps}
-    for name, *args in ORDER:
-        steps[name](*args)
+    for step, *args in ORDER:
+        steps[step](*args)
 
     for copy in copies:
         copy.wait_send()

time: 126 us -> 121 us (0.960)
  Pallas kernels: 123 us -> 117 us
    pallas_call x1, Pallas kernels: 123 us -> 117 us  [per_device(): pl.pallas_call(kernel, out_shape=jax.ShapeDtypeStruct(weights.shape, f32)...]
where the time goes in v3:
time: 121 us; the launch traced here: 120 us
  Pallas kernels  117 us (97%)
  other arithmetic  1.45 us (1%)
    pallas_call x1, Pallas kernels, per_device(): pl.pallas_call(kernel, out_shape=jax.ShapeDtypeStruct(weights.shape, f32)...  117 us

profile of v3, /device:TPU:1, one launch (start us, length us, event | category | flops | bytes accessed | tf_op | source)
XLA Modules:
  0.0 120.4 jit_solution(5809798979298221738)
XLA Ops:
  0.6 0.0 copy-start
  0.6 1.1 copy-done
  1.7 0.0 copy-start.1
  1.7 117.2 %shard_map.41 = f32[1,288,1152]{2,1,0:T(8,128)S(1)} custom-call(bf16[1,288,1152]{2,1,0:T(8,128)(2,1)S(1)} %copy-done), custom_call_target="tpu_custom_call" | custom-call | flops 9200000000 | bytes 4000000 | tf_op jit(solution)/shard_map/pallas_call | solution.py:312
  119.0 0.0 copy-done.1
  119.0 1.4 %multiply_subtract_fusion = (f32[1,288,1152]{2,1,0:T(8,128)}, bf16[1,288,1152]{2,1,0:T(8,128)(2,1)}) fusion(f32[1,288,1152]{2,1,0:T(8,128)S(1)} %copy-done.1, f32[1,288,1152]{2,1,0:T(8,128)S(1)} %shard_map.41), kind=kLoop, calls=%fused_computation | loop fusion | flops 1327104 | bytes 4644864 | tf_op jit(solution)/shard_map/sub | solution.py:344
Async XLA Ops:
  0.6 1.1 copy-start
  1.7 117.2 %copy-start.1 = (f32[1,288,1152]{2,1,0:T(8,128)S(1)}, f32[1,288,1152]{2,1,0:T(8,128)}, u32[]{:S(2)}) copy-start(f32[1,288,1152]{2,1,0:T(8,128)} %param.3) | copy-start | bytes 3981316

commit v4 on v3

--- a/solution.py
+++ b/solution.py
@@ -29,7 +29,7 @@
 }
 
 UNITS = ((0, 0, 512), (0, 512, 512), (0, 1024, 512), (1, 0, 512), (1, 512, 512), (1, 1024, 512), (1, 1536, 512), (1, 2048, 256), (0, 1536, 512), (0, 2048, 256))
-CHUNKS = (128, 256, 256, 256, 256)
+CHUNKS = (256, 256, 256, 384)
 N_COPIES = 256
 
 HOPS = (4, 3)
@@ -41,33 +41,31 @@
 ORDER = (
     (X_OWN,), (X_HAVE, 0), (GRAM, 0), (RS_FIRST, 0), (RS_STEP, 0, 1), (X_UP, 0), (X_DOWN, 1), (RS_STEP, 0, 2),
     (X_HAVE, 2), (GRAM, 1), (RS_FIRST, 1), (RS_STEP, 0, 3), (X_UP, 1), (X_DOWN, 0), (X_HAVE, 1),
-    (RS_STEP, 1, 1), (GRAM, 3), (RS_FIRST, 3), (RS_LAST, 0), (GRAM, 4), (RS_FIRST, 4), (X_HAVE, 3), (GRAM, 5),
-    (RS_FIRST, 5), (RS_STEP, 1, 2), (GRAM, 2), (X_FAR, 0), (RS_STEP, 3, 1), (RS_FIRST, 2), (X_FAR, 1),
-    (RS_STEP, 4, 1), (RS_STEP, 5, 1), (RS_STEP, 1, 3), (X_HAVE, 4), (GRAM, 7), (RS_FIRST, 7), (RS_STEP, 3, 2),
-    (GRAM, 6), (RS_FIRST, 6), (RS_STEP, 2, 1), (RS_STEP, 4, 2), (RS_LAST, 1), (GRAM, 8), (RS_STEP, 7, 1),
-    (RS_STEP, 5, 2), (RS_STEP, 3, 3), (RS_FIRST, 8), (GRAM, 9), (RS_FIRST, 9), (RS_STEP, 6, 1),
-    (RS_STEP, 4, 3), (RS_STEP, 2, 2), (RS_STEP, 5, 3), (AG_FIRST, 0), (RS_STEP, 7, 2), (RS_LAST, 3),
-    (RS_STEP, 8, 1), (RS_STEP, 9, 1), (RS_LAST, 4), (RS_STEP, 6, 2), (RS_STEP, 2, 3), (AG_FIRST, 3),
-    (RS_LAST, 5), (RS_STEP, 7, 3), (AG_STEP, 0, 1), (AG_FIRST, 4), (RS_STEP, 8, 2), (RS_STEP, 6, 3),
-    (RS_STEP, 9, 2), (RS_LAST, 2), (RS_LAST, 7), (AG_STEP, 3, 1), (AG_STEP, 0, 2), (RS_STEP, 8, 3),
-    (AG_STEP, 4, 1), (RS_LAST, 6), (AG_FIRST, 7), (AG_FIRST, 5), (RS_STEP, 9, 3), (AG_STEP, 3, 2),
-    (RS_LAST, 8), (AG_STEP, 0, 3), (AG_FIRST, 6), (AG_STEP, 4, 2), (AG_STEP, 7, 1), (RS_LAST, 9),
-    (AG_STEP, 5, 1), (AG_FIRST, 8), (AG_STEP, 0, 4), (ASSEMBLE, 0), (AG_STEP, 3, 3), (AG_STEP, 6, 1),
-    (AG_FIRST, 9), (AG_STEP, 4, 3), (AG_STEP, 7, 2), (AG_STEP, 5, 2), (AG_FIRST, 2), (AG_FIRST, 1),
-    (AG_STEP, 3, 4), (AG_STEP, 8, 1), (ASSEMBLE, 3), (AG_STEP, 6, 2), (AG_STEP, 9, 1), (AG_STEP, 4, 4),
-    (ASSEMBLE, 4), (AG_STEP, 7, 3), (AG_STEP, 5, 3), (AG_STEP, 2, 1), (AG_STEP, 1, 1), (AG_STEP, 8, 2),
-    (AG_STEP, 7, 4), (ASSEMBLE, 7), (AG_STEP, 6, 3), (AG_STEP, 5, 4), (ASSEMBLE, 5), (AG_STEP, 9, 2),
-    (AG_STEP, 2, 2), (AG_STEP, 1, 2), (AG_STEP, 6, 4), (ASSEMBLE, 6), (AG_STEP, 8, 3), (Y_PARTNER, 0),
-    (Y_PARTNER, 1), (AG_STEP, 9, 3), (AG_STEP, 2, 3), (Y_PARTNER, 2), (AG_STEP, 1, 3), (Y_PARTNER, 3),
-    (AG_STEP, 8, 4), (ASSEMBLE, 8), (Y_PARTNER, 4), (AG_STEP, 9, 4), (ASSEMBLE, 9), (AG_STEP, 2, 4),
-    (ASSEMBLE, 2), (AG_STEP, 1, 4), (ASSEMBLE, 1), (Y_OWN, 0), (V_OWN, 0), (Y_OWN, 1), (V_OWN, 1), (Y_OWN, 2),
-    (Y_OWN, 3), (Y_OWN, 4), (V_UP, 0, 0), (V_UP, 1, 0), (V_DOWN, 1, 0), (V_DOWN, 0, 0), (V_OWN, 2),
-    (V_UP, 0, 1), (V_DOWN, 1, 1), (V_UP, 1, 1), (V_DOWN, 0, 1), (V_OWN, 3), (V_FAR, 0, 0), (V_FAR, 1, 0),
-    (V_UP, 0, 2), (V_DOWN, 1, 2), (Z_BOTH, 0), (V_DOWN, 0, 2), (V_OWN, 4), (V_UP, 1, 2), (V_FAR, 0, 1),
-    (V_FAR, 1, 1), (V_UP, 0, 3), (V_DOWN, 1, 3), (Z_BOTH, 1), (V_DOWN, 0, 3), (V_UP, 1, 3), (FINISH, 0),
-    (V_FAR, 0, 2), (V_FAR, 1, 2), (V_UP, 0, 4), (V_DOWN, 1, 4), (Z_BOTH, 2), (V_DOWN, 0, 4), (V_UP, 1, 4),
-    (V_FAR, 0, 3), (V_FAR, 1, 3), (FINISH, 1), (V_FAR, 0, 4), (V_FAR, 1, 4), (Z_BOTH, 3), (Z_BOTH, 4),
-    (FINISH, 2), (FINISH, 3), (FINISH, 4),
+    (RS_STEP, 1, 1), (GRAM, 4), (RS_FIRST, 4), (GRAM, 3), (X_HAVE, 3), (RS_FIRST, 3), (GRAM, 5), (RS_FIRST, 5),
+    (RS_STEP, 1, 2), (RS_LAST, 0), (GRAM, 2), (X_FAR, 0), (X_FAR, 1), (RS_STEP, 4, 1), (RS_FIRST, 2),
+    (RS_STEP, 3, 1), (RS_STEP, 5, 1), (RS_STEP, 1, 3), (X_HAVE, 4), (GRAM, 6), (RS_STEP, 4, 2), (RS_FIRST, 6),
+    (RS_STEP, 2, 1), (GRAM, 7), (RS_FIRST, 7), (RS_STEP, 3, 2), (GRAM, 9), (RS_LAST, 1), (AG_FIRST, 0),
+    (GRAM, 8), (RS_STEP, 4, 3), (RS_STEP, 5, 2), (RS_STEP, 6, 1), (RS_FIRST, 8), (RS_STEP, 2, 2),
+    (RS_STEP, 3, 3), (RS_STEP, 7, 1), (RS_LAST, 4), (RS_FIRST, 9), (AG_STEP, 0, 1), (RS_STEP, 5, 3),
+    (RS_STEP, 6, 2), (RS_STEP, 2, 3), (AG_FIRST, 4), (RS_LAST, 3), (RS_STEP, 8, 1), (RS_STEP, 7, 2),
+    (RS_STEP, 9, 1), (RS_LAST, 5), (AG_STEP, 0, 2), (RS_STEP, 6, 3), (AG_FIRST, 3), (RS_LAST, 2),
+    (AG_STEP, 4, 1), (RS_STEP, 7, 3), (AG_FIRST, 5), (RS_STEP, 8, 2), (RS_STEP, 9, 2), (AG_FIRST, 2),
+    (RS_LAST, 6), (AG_STEP, 0, 3), (AG_STEP, 3, 1), (RS_LAST, 7), (AG_STEP, 4, 2), (RS_STEP, 8, 3),
+    (AG_STEP, 5, 1), (AG_FIRST, 6), (RS_STEP, 9, 3), (AG_FIRST, 7), (AG_STEP, 0, 4), (ASSEMBLE, 0),
+    (AG_STEP, 2, 1), (AG_STEP, 3, 2), (RS_LAST, 8), (AG_STEP, 4, 3), (AG_STEP, 5, 2), (RS_LAST, 9),
+    (AG_STEP, 6, 1), (AG_STEP, 7, 1), (AG_FIRST, 8), (AG_STEP, 2, 2), (AG_STEP, 4, 4), (ASSEMBLE, 4),
+    (AG_STEP, 3, 3), (AG_FIRST, 9), (AG_FIRST, 1), (AG_STEP, 5, 3), (AG_STEP, 6, 2), (AG_STEP, 7, 2),
+    (AG_STEP, 8, 1), (AG_STEP, 3, 4), (ASSEMBLE, 3), (AG_STEP, 2, 3), (AG_STEP, 9, 1), (AG_STEP, 5, 4),
+    (ASSEMBLE, 5), (AG_STEP, 1, 1), (AG_STEP, 6, 3), (AG_STEP, 7, 3), (AG_STEP, 2, 4), (ASSEMBLE, 2),
+    (AG_STEP, 8, 2), (AG_STEP, 9, 2), (AG_STEP, 1, 2), (AG_STEP, 6, 4), (ASSEMBLE, 6), (AG_STEP, 7, 4),
+    (ASSEMBLE, 7), (Y_PARTNER, 0), (Y_PARTNER, 1), (AG_STEP, 8, 3), (AG_STEP, 9, 3), (Y_PARTNER, 2),
+    (AG_STEP, 1, 3), (Y_PARTNER, 3), (AG_STEP, 8, 4), (ASSEMBLE, 8), (AG_STEP, 9, 4), (ASSEMBLE, 9),
+    (AG_STEP, 1, 4), (ASSEMBLE, 1), (Y_OWN, 0), (V_OWN, 0), (Y_OWN, 1), (Y_OWN, 2), (Y_OWN, 3), (V_OWN, 1),
+    (V_UP, 0, 0), (V_DOWN, 1, 0), (V_UP, 1, 0), (V_DOWN, 0, 0), (V_OWN, 2), (V_UP, 0, 1), (V_DOWN, 1, 1),
+    (V_UP, 1, 1), (V_DOWN, 0, 1), (V_FAR, 0, 0), (V_FAR, 1, 0), (V_OWN, 3), (V_UP, 0, 2), (V_DOWN, 1, 2),
+    (Z_BOTH, 0), (V_DOWN, 0, 2), (V_UP, 1, 2), (V_FAR, 0, 1), (V_FAR, 1, 1), (Z_BOTH, 1), (V_UP, 0, 3),
+    (V_DOWN, 1, 3), (V_UP, 1, 3), (V_DOWN, 0, 3), (FINISH, 0), (V_FAR, 0, 2), (V_FAR, 1, 2), (Z_BOTH, 2),
+    (V_FAR, 1, 3), (V_FAR, 0, 3), (FINISH, 1), (Z_BOTH, 3), (FINISH, 2), (FINISH, 3),
 )
 
 

time: 121 us -> 123 us (1.017)
  Pallas kernels: 117 us -> 119 us
    pallas_call x1, Pallas kernels: 117 us -> 119 us  [per_device(): pl.pallas_call(kernel, out_shape=jax.ShapeDtypeStruct(weights.shape, f32)...]
where the time goes in v4:
time: 123 us
  Pallas kernels  119 us (97%)
  other arithmetic  1.45 us (1%)
    pallas_call x1, Pallas kernels, per_device(): pl.pallas_call(kernel, out_shape=jax.ShapeDtypeStruct(weights.shape, f32)...  119 us

profile of v4, /device:TPU:1, one launch (start us, length us, event | category | flops | bytes accessed | tf_op | source)
XLA Modules:
  0.0 122.6 jit_solution(7000604800165820082)
XLA Ops:
  0.6 0.0 copy-start
  0.6 1.1 copy-done
  1.7 0.0 copy-start.1
  1.7 119.4 %shard_map.41 = f32[1,288,1152]{2,1,0:T(8,128)S(1)} custom-call(bf16[1,288,1152]{2,1,0:T(8,128)(2,1)S(1)} %copy-done), custom_call_target="tpu_custom_call" | custom-call | flops 9200000000 | bytes 4000000 | tf_op jit(solution)/shard_map/pallas_call | solution.py:310
  121.1 0.0 copy-done.1
  121.1 1.4 %multiply_subtract_fusion = (f32[1,288,1152]{2,1,0:T(8,128)}, bf16[1,288,1152]{2,1,0:T(8,128)(2,1)}) fusion(f32[1,288,1152]{2,1,0:T(8,128)S(1)} %copy-done.1, f32[1,288,1152]{2,1,0:T(8,128)S(1)} %shard_map.41), kind=kLoop, calls=%fused_computation | loop fusion | flops 1327104 | bytes 4644864 | tf_op jit(solution)/shard_map/sub | solution.py:342
Async XLA Ops:
  0.6 1.1 copy-start
  1.7 119.4 %copy-start.1 = (f32[1,288,1152]{2,1,0:T(8,128)S(1)}, f32[1,288,1152]{2,1,0:T(8,128)}, u32[]{:S(2)}) copy-start(f32[1,288,1152]{2,1,0:T(8,128)} %param.3) | copy-start | bytes 3981316
